TPU v7x, 32 devices: a whole 2x2x4 slice. The times are simulated.
32 devices in a mesh: dp: 32 (over z, y, x, core).
Axes of the slice: x: 2, y: 2, z: 4, core: 2. Of those that a mesh axis runs over, the one named last changes fastest.
Arguments:
- inputs: bfloat16 [3, 32768, 384], P(None, 'dp'), may hold values from -6 to 6
- cotangent: bfloat16 [3, 32768, 384], P(None, 'dp'), may hold values from -6 to 6
- w_qkv: bfloat16 [384, 1152], P('dp'), may hold values from -0.3125 to 0.3125
- w_out: bfloat16 [384, 384], P('dp'), may hold values from -0.875 to 0.875
- w_fc1: bfloat16 [384, 1536], P('dp'), may hold values from -0.3125 to 0.3125
- w_fc2: bfloat16 [1536, 384], P('dp'), may hold values from -0.15625 to 0.15625
- norm1_gain: bfloat16 [384], P('dp'), may hold values from 0.5 to 1.5
- norm1_bias: bfloat16 [384], P('dp'), may hold values from -4 to 4
- query_bias: bfloat16 [384], P('dp'), may hold values from -6 to 6
- value_bias: bfloat16 [384], P('dp'), may hold values from -6 to 6
- out_bias: bfloat16 [384], P('dp'), may hold values from -4 to 4
- norm2_gain: bfloat16 [384], P('dp'), may hold values from 0.5 to 1.5
- norm2_bias: bfloat16 [384], P('dp'), may hold values from -4 to 4
- fc1_bias: bfloat16 [1536], P('dp'), may hold values from -6 to 6
- fc2_bias: bfloat16 [384], P('dp'), may hold values from -4 to 4
- image_tokens: int32 [3, 32], replicated, may hold values from 102 to 326, as said below
- image_count: int32 [3, 32], replicated, may hold values from 2 to 10, as said below
Outputs:
- outputs: bfloat16 [3, 32768, 384], P(None, 'dp')
- input_grad: bfloat16 [3, 32768, 384], P(None, 'dp')
- grad_qkv: float32 [384, 1152], P('dp')
- grad_out: float32 [384, 384], P('dp')
- grad_fc1: float32 [384, 1536], P('dp')
- grad_fc2: float32 [1536, 384], P('dp')
- grad_norm1_gain: float32 [384], P('dp')
- grad_norm1_bias: float32 [384], P('dp')
- grad_query_bias: float32 [384], P('dp')
- grad_value_bias: float32 [384], P('dp')
- grad_out_bias: float32 [384], P('dp')
- grad_norm2_gain: float32 [384], P('dp')
- grad_norm2_bias: float32 [384], P('dp')
- grad_fc1_bias: float32 [1536], P('dp')
- grad_fc2_bias: float32 [384], P('dp')
Inputs may be any that keep to these rules, and one draw needn't show every extreme that they name: `image_tokens`: each entry is one of 102, 198, 326. image_count times the matching image_tokens entry is at most 1024; the images fill the first slots of their block.
All inputs are finite; a program needn't handle non-finite values.
Results may differ from a plain program's by a relative error of at most 0.012.
Values may be sent and summed in bfloat16 or wider, within the bound.
A program may use at most 192 MiB of HBM per device.

v0:
```python
import functools

import jax
import jax.numpy as jnp
from jax import lax
from jax.experimental import pallas as pl
from jax.experimental.pallas import tpu as pltpu
from jax.sharding import PartitionSpec as P

F32, BF16 = jnp.float32, jnp.bfloat16
MESH = pl.DeviceIdType.MESH

HEADS = 6
EPS = 1e-06
FAR = -1e30
V_GAIN1, V_SHIFT1, V_QKV, V_OUT, V_GAIN2, V_SHIFT2, V_FC1, V_FC2 = range(8)
G_GAIN1, G_SHIFT1, G_QKV, G_OUT, G_GAIN2, G_SHIFT2, G_FC1, G_FC2 = range(8)


def mm(a, b):
    return jnp.dot(a, b, preferred_element_type=F32)

def mm_t(a, b):
    return lax.dot_general(a, b, (((1,), (1,)), ((), ())), preferred_element_type=F32)

def t_mm(a, b):
    return lax.dot_general(a, b, (((0,), (0,)), ((), ())), preferred_element_type=F32)


def norm_rows(v):
    width = v.shape[1]
    off = v - jnp.sum(v, axis=1, keepdims=True) * (1.0 / width)
    inv = lax.rsqrt(jnp.sum(off * off, axis=1, keepdims=True) * (1.0 / width) + EPS)
    return off * inv, inv


def norm_back(n, inv, t):
    width = n.shape[1]
    a = jnp.sum(t, axis=1, keepdims=True) * (1.0 / width)
    b = jnp.sum(t * n, axis=1, keepdims=True) * (1.0 / width)
    return inv * (t - a - n * b)


def col_sum(v):
    return jnp.sum(v, axis=0, keepdims=True)


def images_per_window(length):
    return jnp.where(length <= 128, 2, 1)


def window(meta, w, wq, wk, rows):
    length, count = meta
    group = images_per_window(length)
    lo = w * (length * group)
    hi = jnp.minimum(lo + length * group, length * count)
    base = (lo // 16) * 16
    sq = pl.multiple_of(jnp.minimum(base, rows - wq), 16)
    sk = pl.multiple_of(jnp.minimum(base, rows - wk), 16)
    return lo, hi, length, sq, sk


def seg_of(start, n, lo, hi, length):
    r = start + lax.broadcasted_iota(jnp.int32, (n, 128), 0)
    inside = jnp.logical_and(r >= lo, r < hi)
    return inside, jnp.where(inside, jnp.where(r >= lo + length, 1, 0), 2)


def halves(v):
    left = lax.broadcasted_iota(jnp.int32, v.shape, 1) < 64
    zero = jnp.zeros_like(v)
    return jnp.where(left, v, zero), jnp.where(left, zero, v)


def attend_fwd(meta, qkv_s, o_s, inv_s, e_s, wq, wk, pairs, width):
    rows = qkv_s.shape[0]
    scale = 0.125 * 1.4426950408889634

    def one(w, carry):
        lo, hi, length, sq, sk = window(meta, w, wq, wk, rows)
        in_q, seg_q = seg_of(sq, wq, lo, hi, length)
        _, seg_k = seg_of(sk, wk, lo, hi, length)
        lane_q = lax.broadcasted_iota(jnp.int32, (wq, 128), 1)
        lane_k = lax.broadcasted_iota(jnp.int32, (wk, 128), 1)
        aug_q = jnp.where(jnp.logical_and(lane_q != seg_q, lane_q < 3), 1.0, 0.0).astype(BF16)
        aug_k = jnp.where(lane_k == seg_k, FAR, 0.0).astype(BF16)
        ones0 = jnp.where(lane_k < 64, 1.0, 0.0).astype(BF16)
        ones1 = jnp.where(lane_k < 64, 0.0, 1.0).astype(BF16)
        for p in range(pairs):
            c = 128 * p
            q2 = qkv_s[pl.ds(sq, wq), c : c + 128]
            k0, k1 = halves(qkv_s[pl.ds(sk, wk), width + c : width + c + 128])
            v0, v1 = halves(qkv_s[pl.ds(sk, wk), 2 * width + c : 2 * width + c + 128])
            left = jnp.concatenate([q2, aug_q], axis=1)
            right = jnp.concatenate(
                [jnp.concatenate([k0, aug_k], axis=1), jnp.concatenate([k1, aug_k], axis=1)], axis=0
            )
            s = mm_t(left, right)
            parts = []
            for h in range(2):
                sh = s[:, h * wk : (h + 1) * wk]
                top = jnp.max(sh, axis=1, keepdims=True)
                parts.append(jnp.exp2((sh - top) * scale).astype(BF16))
            e = jnp.concatenate(parts, axis=1)
            e_s[w * pairs + p] = e
            vals = jnp.concatenate(
                [jnp.concatenate([v0, ones0], axis=1), jnp.concatenate([v1, ones1], axis=1)], axis=0
            )
            both = mm(e, vals)
            inv = 1.0 / both[:, 128:]
            o = (both[:, :128] * inv).astype(BF16)
            dst = (pl.ds(sq, wq), pl.ds(c, 128))
            o_s[dst] = jnp.where(in_q, o, o_s[dst])
            inv_s[dst] = jnp.where(in_q, inv, inv_s[dst])
        return carry

    length, count = meta
    lax.fori_loop(0, jnp.where(length <= 128, (count + 1) // 2, count), one, 0)


def attend_bwd(meta, qkv_s, o_s, inv_s, e_s, go_s, gqkv_s, wq, wk, pairs, width):
    rows = qkv_s.shape[0]

    def one(w, carry):
        lo, hi, length, sq, sk = window(meta, w, wq, wk, rows)
        in_q, _ = seg_of(sq, wq, lo, hi, length)
        in_k, _ = seg_of(sk, wk, lo, hi, length)
        for p in range(pairs):
            c = 128 * p
            e = e_s[w * pairs + p]
            q0, q1 = halves(qkv_s[pl.ds(sq, wq), c : c + 128])
            k0, k1 = halves(qkv_s[pl.ds(sk, wk), width + c : width + c + 128])
            v0, v1 = halves(qkv_s[pl.ds(sk, wk), 2 * width + c : 2 * width + c + 128])
            dst_q = (pl.ds(sq, wq), pl.ds(c, 128))
            go = (go_s[dst_q].astype(F32) * inv_s[dst_q]).astype(BF16)
            prod0, prod1 = halves(go.astype(F32) * o_s[dst_q].astype(F32))
            d = (jnp.sum(prod0, axis=1, keepdims=True), jnp.sum(prod1, axis=1, keepdims=True))
            gp = mm_t(go, jnp.concatenate([v0, v1], axis=0))
            gs = []
            for h in range(2):
                sl = slice(h * wk, (h + 1) * wk)
                gs.append((e[:, sl].astype(F32) * (gp[:, sl] - d[h])).astype(BF16))
            gq = mm(jnp.concatenate(gs, axis=1), jnp.concatenate([k0, k1], axis=0)) * 0.125
            gk = t_mm(jnp.concatenate(gs, axis=0), jnp.concatenate([q0, q1], axis=0)) * 0.125
            gv = t_mm(
                jnp.concatenate([e[:, :wk], e[:, wk:]], axis=0), jnp.concatenate(halves(go), axis=0)
            )
            gqkv_s[dst_q] = jnp.where(in_q, gq.astype(BF16), gqkv_s[dst_q])
            dst_k = (pl.ds(sk, wk), pl.ds(width + c, 128))
            gqkv_s[dst_k] = jnp.where(in_k, gk.astype(BF16), gqkv_s[dst_k])
            dst_v = (pl.ds(sk, wk), pl.ds(2 * width + c, 128))
            gqkv_s[dst_v] = jnp.where(in_k, gv.astype(BF16), gqkv_s[dst_v])
        return carry

    length, count = meta
    lax.fori_loop(0, jnp.where(length <= 128, (count + 1) // 2, count), one, 0)


WIDE = (352, 384)
NARROW = (224, 256)


def fold_matrix(part, count, high):
    rows, cols = 4 * count * part, count * high
    r = lax.broadcasted_iota(jnp.int32, (rows, cols), 0).astype(F32)
    c = lax.broadcasted_iota(jnp.int32, (rows, cols), 1).astype(F32)
    block = jnp.floor((c + 0.5) * (1.0 / high))
    inner = c - block * high
    piece = jnp.floor((inner + 0.5) * (1.0 / part))
    want = piece * (count * part) + block * part + (inner - piece * part)
    return jnp.where(jnp.logical_and(want == r, piece < 4), 1.0, 0.0).astype(BF16)


def unfold(blocks, dsts, part, high):
    count = 96 // part
    pick = fold_matrix(part, count, high)
    for t in range(len(blocks) // count):
        group = jnp.concatenate([blocks[j][...] for j in range(t * count, (t + 1) * count)], axis=0)
        full = mm(pick, group).astype(BF16)
        for a in range(4):
            dsts[a][96 * t : 96 * (t + 1), :] = full[96 * a : 96 * (a + 1), :]


def fold(srcs, blocks, part, high):
    count = 96 // part
    pick = fold_matrix(part, count, high)
    for t in range(len(blocks) // count):
        rows = slice(96 * t, 96 * (t + 1))
        four = jnp.concatenate([s[rows, :].astype(BF16) for s in srcs], axis=0)
        full = t_mm(pick, four).astype(BF16)
        for i in range(count):
            blocks[t * count + i][...] = full[i * high : (i + 1) * high, :]


def unfold_vectors(blocks, vec, part):
    n = len(blocks)
    width = part * n
    lane = lax.broadcasted_iota(jnp.int32, (8, 128), 1)
    total = jnp.zeros((8, width), F32)
    wide = jnp.zeros((8, 4 * width), F32)
    for j in range(n):
        pair = blocks[j][...].astype(F32)
        one = jnp.where(lane < part, pair[0:8], 0.0)
        one = jnp.concatenate([one, jnp.zeros((8, width - 128), F32)], axis=1)
        total = total + pltpu.roll(one, j * part, 1)
        one = jnp.where(lane < 4 * part, pair[8:16], 0.0)
        one = jnp.concatenate([one, jnp.zeros((8, 4 * width - 128), F32)], axis=1)
        wide = wide + pltpu.roll(one, 4 * j * part, 1)
    vec[...] = jnp.zeros_like(vec)
    for i, (row, col) in enumerate(VECTORS):
        vec[row : row + 1, col * width : (col + 1) * width] = total[i : i + 1]
    vec[V_FC1 : V_FC1 + 1, :] = wide[0:1]


def fold_vectors(vec, blocks, part):
    n = len(blocks)
    width = part * n
    eight = jnp.concatenate(
        [vec[row : row + 1, col * width : (col + 1) * width] for row, col in VECTORS], axis=0
    )
    wide = jnp.broadcast_to(vec[V_FC1 : V_FC1 + 1, :], (8, 4 * width))
    for j in range(n):
        blocks[j][0:8, :] = pltpu.roll(eight, (width - j * part) % width, 1)[:, :128]
        blocks[j][8:16, :] = pltpu.roll(wide, (4 * width - 4 * j * part) % (4 * width), 1)[:, :128]


VECTORS = ((V_GAIN1, 0), (V_SHIFT1, 0), (V_QKV, 0), (V_QKV, 2), (V_OUT, 0), (V_GAIN2, 0), (V_SHIFT2, 0), (V_FC2, 0))


def layer_kernel(
    tokens, counts, x_ref, cot_ref, qkv_ref, wout, w1, w2, vec,
    out_ref, gqkv_ref, gmix_ref, p_fc1, p_fc2, a_out, a_vec,
    a_fc1, a_fc2, o_s, inv_s, e1_s, e2_s, h2_s, act_s, gpre_s, gy_s, gb_s, go_s,
    part, phases=("af", "mlp", "wg", "ab"), tile=512, chunk=256,
):
    m = pl.program_id(0)
    me = lax.axis_index("dp")
    rows, width = x_ref.shape[1], x_ref.shape[2]
    hidden = w1.shape[1]
    pairs = HEADS // 2
    length, count = tokens[m, me], counts[m, me]
    meta = (length, count)
    total = length * count
    qkv_s, gqkv_s, gmix_s = qkv_ref.at[0], gqkv_ref.at[0], gmix_ref.at[0]

    @pl.when(m == 0)
    def _():
        for ref in (a_out, a_fc1, a_fc2, a_vec):
            ref[...] = jnp.zeros_like(ref)

    def v(i, n=width):
        return vec[i : i + 1, 0:n]

    def add_vec(i, val):
        a_vec[i : i + 1, 0 : val.shape[1]] += val

    o_s[...] = qkv_s[:, 2 * width :]

    if "af" in phases:
        fwd = functools.partial(attend_fwd, meta, qkv_s, o_s, inv_s)
        @pl.when(length > 256)
        def _():
            fwd(e1_s, *WIDE, pairs, width)
        @pl.when(length <= 256)
        def _():
            fwd(e2_s, *NARROW, pairs, width)

    if "mlp" in phases:
        def mlp(i, c):
            r = pl.ds(pl.multiple_of(i * tile, tile), tile)
            valid = (i * tile + lax.broadcasted_iota(jnp.int32, (tile, 1), 0)) < total
            mixed = x_ref[0, r, :].astype(F32) + mm(o_s[r, :], wout[...]) + v(V_OUT)
            n2, r2 = norm_rows(mixed)
            h2 = (n2 * v(V_GAIN2) + v(V_SHIFT2)).astype(BF16)
            h2_s[r, :] = h2
            gy = jnp.where(valid, cot_ref[0, r, :].astype(F32), 0.0)
            gyl = gy.astype(BF16)
            gy_s[r, :] = gyl
            add_vec(G_FC2, col_sum(gy))
            for f in range(0, hidden, chunk):
                fs = slice(f, f + chunk)
                pre = mm(h2, w1[:, fs]) + vec[V_FC1 : V_FC1 + 1, fs]
                cdf = 0.5 * lax.erf(pre * 0.7071067811865476) + 0.5
                act_s[r, fs] = (pre * cdf).astype(BF16)
                slope = cdf + pre * (jnp.exp(pre * pre * -0.5) * 0.3989422804014327)
                gpre = (slope * mm_t(gyl, w2[fs, :])).astype(BF16)
                gpre_s[r, fs] = gpre
                a_vec[G_FC1 : G_FC1 + 1, fs] += col_sum(gpre.astype(F32))
            final = mixed + mm(act_s[r, :], w2[...]) + v(V_FC2)
            out_ref[0, r, :] = jnp.where(valid, final, 0.0).astype(BF16)
            gh2 = mm_t(gpre_s[r, :], w1[...])
            add_vec(G_GAIN2, col_sum(gh2 * n2))
            add_vec(G_SHIFT2, col_sum(gh2))
            gmix = gy + norm_back(n2, r2, gh2 * v(V_GAIN2))
            gmix_s[r, :] = gmix
            gb = gmix.astype(BF16)
            gb_s[r, :] = gb
            add_vec(G_OUT, col_sum(gb.astype(F32)))
            go_s[r, :] = mm_t(gb, wout[...]).astype(BF16)
            return c
        lax.fori_loop(0, rows // tile, mlp, 0)

    if "wg" in phases:
        a_fc1[...] += t_mm(h2_s[...], gpre_s[...])
        a_fc2[...] += t_mm(act_s[...], gy_s[...])
        a_out[...] += t_mm(o_s[...], gb_s[...])

    gqkv_s[:, : 2 * width] = jnp.zeros((rows, 2 * width), BF16)
    gqkv_s[:, 2 * width :] = go_s[...]

    if "ab" in phases:
        bwd = functools.partial(attend_bwd, meta, qkv_s, o_s, inv_s)
        @pl.when(length > 256)
        def _():
            bwd(e1_s, go_s, gqkv_s, *WIDE, pairs, width)
        @pl.when(length <= 256)
        def _():
            bwd(e2_s, go_s, gqkv_s, *NARROW, pairs, width)

    @pl.when(m == pl.num_programs(0) - 1)
    def _():
        high = p_fc1.shape[0] // (width // part)
        blocks = [p_fc1.at[j * high : (j + 1) * high, :] for j in range(width // part)]
        fold([a_fc1.at[:, i * width : (i + 1) * width] for i in range(4)], blocks, part, high)
        p_fc2[...] = a_fc2[...].astype(BF16)


def layer_call(tokens, counts, x, cot, qkv, wout, w1, w2, vec, n, **kw):
    micro, rows, width = x.shape
    hidden = w2.shape[0]
    part = width // n
    high = -(-4 * part // 16) * 16
    def per_step(cols):
        return pl.BlockSpec((1, rows, cols), lambda m: (m, 0, 0))
    def whole(shape):
        return pl.BlockSpec(shape, lambda m: (0, 0), pipeline_mode=pl.Buffered(1))
    bf = lambda n: pltpu.VMEM((rows, n), BF16)
    outs = [(x.shape, BF16), ((micro, rows, 3 * width), BF16), (x.shape, F32)]
    kept = [((n * high, width), BF16), ((hidden, width), BF16), ((width, width), F32), (vec.shape, F32)]
    return pl.pallas_call(
        functools.partial(layer_kernel, part=part, **kw),
        grid=(micro,),
        in_specs=[pl.BlockSpec(memory_space=pltpu.SMEM)] * 2 + [per_step(width), per_step(width), per_step(3 * width)]
        + [whole(a.shape) for a in (wout, w1, w2, vec)],
        out_specs=[per_step(s[2]) for s, _ in outs] + [whole(s) for s, _ in kept],
        out_shape=[jax.ShapeDtypeStruct(s, d) for s, d in outs + kept],
        scratch_shapes=[
            pltpu.VMEM((width, hidden), F32), pltpu.VMEM((hidden, width), F32),
            bf(width), pltpu.VMEM((rows, width), F32),
            pltpu.VMEM((9, 352, 768), BF16), pltpu.VMEM((15, 224, 512), BF16),
            bf(width), bf(hidden), bf(hidden), bf(width), bf(width), bf(width),
        ],
        compiler_params=pltpu.CompilerParams(vmem_limit_bytes=64 * 2**20 - 2**17),
    )(tokens, counts, x, cot, qkv, wout, w1, w2, vec)


def bit_of(me, b):
    return (me // (1 << b)) % 2


class Place:
    def __init__(self, n):
        self.me = lax.axis_index("dp")
        self.count = n // 8
        self.z, self.y, self.x, self.c = self.me // 8, bit_of(self.me, 2), bit_of(self.me, 1), bit_of(self.me, 0)
        self.over_y = self.me + 4 * (1 - 2 * self.y)
        self.over_x = self.me + 2 * (1 - 2 * self.x)
        self.twin = self.me + (1 - 2 * self.c)
        self.steps = sorted(range(1, self.count), key=lambda k: min(k, self.count - k))

    def ahead(self, k):
        return (self.z + k) % self.count

    def behind(self, k):
        return (self.z + self.count - k) % self.count

    def at(self, z):
        return self.me + 8 * (z - self.z)

    def meet(self):
        barrier = pltpu.get_barrier_semaphore()
        others = [self.over_y, self.over_x, self.twin] + [self.at(self.ahead(k)) for k in range(1, self.count)]
        for device in others:
            pl.semaphore_signal(barrier, inc=1, device_id=(device,), device_id_type=MESH)
        pl.semaphore_wait(barrier, len(others))


LINE, ALONG_X, ALONG_Y, DIAG_X, DIAG_Y, TWIN = range(6)


class Wire:
    def __init__(self, place, cut, send, recv):
        self.place, self.cut, self.send, self.recv, self.started = place, cut, send, recv, []

    def copy(self, kind, k, src, dst, device):
        return pltpu.make_async_remote_copy(
            src_ref=src, dst_ref=dst, send_sem=self.send.at[kind, k], recv_sem=self.recv.at[kind, k],
            device_id=(device,), device_id_type=MESH)

    def push(self, kind, k, src, dst, device):
        copy = self.copy(kind, k, src, dst, device)
        copy.start()
        self.started.append(copy)

    def arrive(self, kind, k, dst):
        self.copy(kind, k, dst, dst, self.place.twin).wait_recv()

    def finish(self):
        for copy in self.started:
            copy.wait_send()

    def columns(self, k, width):
        if self.cut is None:
            return slice(0, width), None
        cut = 128 if (k + self.cut) % 2 else width - 128
        return slice(0, cut), slice(cut, width)


class Gather(Wire):
    def __init__(self, place, ref, cut, send, recv):
        super().__init__(place, cut, send, recv)
        self.ref = ref

    def block(self, k, over_y, over_x, cols=slice(None)):
        p = self.place
        y = 1 - p.y if over_y else p.y
        x = 1 - p.x if over_x else p.x
        return self.ref.at[p.behind(k), y, x, p.c, :, cols]

    def same(self, kind, k, view, device):
        self.push(kind, k, view, view, device)

    def begin(self):
        p = self.place
        for k in p.steps:
            self.same(LINE, k, self.block(0, False, False), p.at(p.ahead(k)))

    def line(self, k):
        view = self.block(k, False, False)
        if k:
            self.arrive(LINE, k, view)
        self.same(ALONG_X, k, view, self.place.over_x)
        self.same(ALONG_Y, k, view, self.place.over_y)

    def plane(self, k):
        first, second = self.columns(k, self.ref.shape[-1])
        self.arrive(ALONG_X, k, self.block(k, False, True))
        self.same(DIAG_Y, k, self.block(k, False, True, first), self.place.over_y)
        self.arrive(ALONG_Y, k, self.block(k, True, False))
        if second is not None:
            self.same(DIAG_X, k, self.block(k, True, False, second), self.place.over_x)

    def corner(self, k):
        first, second = self.columns(k, self.ref.shape[-1])
        self.arrive(DIAG_Y, k, self.block(k, True, True, first))
        if second is not None:
            self.arrive(DIAG_X, k, self.block(k, True, True, second))
        p = self.place
        self.same(TWIN, k, self.ref.at[p.behind(k), :, :, p.c], p.twin)

    def last(self):
        p = self.place
        for k in range(p.count):
            self.arrive(TWIN, k, self.ref.at[p.behind(k), :, :, 1 - p.c])


class Scatter(Wire):
    def __init__(self, place, src, cut, scratch, out, send, recv):
        super().__init__(place, cut, send, recv)
        self.src, self.out = src, out
        self.twins, self.diag_x, self.diag_y, self.from_x, self.from_y, self.lines, self.sums = scratch

    def half(self, k, y, x):
        p = self.place
        z = p.ahead(k)
        return self.src[z, y, x, p.c].astype(F32) + self.twins[z, y, x].astype(F32)

    def begin(self):
        p = self.place
        for k in p.steps + [0]:
            z = p.ahead(k)
            self.push(TWIN, k, self.src.at[z, :, :, 1 - p.c], self.twins.at[z], p.twin)

    def corner(self, k):
        p = self.place
        self.arrive(TWIN, k, self.twins.at[p.ahead(k)])
        first, second = self.columns(k, self.src.shape[-1])
        held = self.sums.at[0, k]
        held[...] = self.half(k, 1 - p.y, 1 - p.x).astype(held.dtype)
        self.push(DIAG_Y, k, held.at[:, first], self.diag_x.at[k, :, first], p.over_y)
        if second is not None:
            self.push(DIAG_X, k, held.at[:, second], self.diag_y.at[k, :, second], p.over_x)

    def plane(self, k):
        p = self.place
        first, second = self.columns(k, self.src.shape[-1])
        self.arrive(DIAG_Y, k, self.diag_x.at[k, :, first])
        held = self.sums.at[1, k]
        total = self.half(k, p.y, 1 - p.x)
        held[:, first] = (total[:, first] + self.diag_x[k, :, first].astype(F32)).astype(held.dtype)
        if second is not None:
            held[:, second] = total[:, second].astype(held.dtype)
        self.push(ALONG_X, k, held, self.from_x.at[k], p.over_x)
        held = self.sums.at[2, k]
        total = self.half(k, 1 - p.y, p.x)
        if second is None:
            held[...] = total.astype(held.dtype)
        else:
            self.arrive(DIAG_X, k, self.diag_y.at[k, :, second])
            held[:, first] = total[:, first].astype(held.dtype)
            held[:, second] = (total[:, second] + self.diag_y[k, :, second].astype(F32)).astype(held.dtype)
        self.push(ALONG_Y, k, held, self.from_y.at[k], p.over_y)

    def line(self, k):
        p = self.place
        self.arrive(ALONG_X, k, self.from_x.at[k])
        self.arrive(ALONG_Y, k, self.from_y.at[k])
        total = self.half(k, p.y, p.x) + self.from_x[k].astype(F32) + self.from_y[k].astype(F32)
        if k == 0:
            self.out[...] = total
            return
        held = self.sums.at[3, k]
        held[...] = total.astype(held.dtype)
        self.push(LINE, k, held, self.lines.at[k], p.at(p.ahead(k)))

    def last(self):
        total = self.out[...]
        for k in self.place.steps:
            self.arrive(LINE, k, self.lines.at[k])
            total = total + self.lines[k].astype(F32)
        self.out[...] = total


def gather_kernel(
    n, tile, x_ref, w_qkv, w_out, w_fc1, w_fc2, *refs,
):
    small = refs[:9]
    qkv_ref, wqkv, wout, w1, g_fc2, vec, x_s, qkv_s, g_attn, g_fc1, g_vec, pad, pad_vec, x_sem, qkv_sem, send, recv = refs[9:]
    place = Place(n)
    micro, rows, width = x_s.shape
    part = width // n
    height = g_fc1.shape[-2]
    loads = [pltpu.make_async_copy(x_ref.at[m], x_s.at[m], x_sem.at[m]) for m in range(micro)]
    for load in loads:
        load.start()
    own = (place.z, place.y, place.x, place.c)
    if height > 4 * part:
        pad[...] = jnp.zeros_like(pad)
    pad_vec[...] = jnp.zeros_like(pad_vec)
    for i in range(8):
        pad_vec[i : i + 1, 0:part] = small[i][...].astype(F32).reshape(1, part)
    pad_vec[8:9, 0 : 4 * part] = small[8][...].astype(F32).reshape(1, 4 * part)
    g_vec[own] = pad_vec[...].astype(BF16)
    def fold_own(dst, four):
        for a, piece in enumerate(four):
            pad[a * part : (a + 1) * part, :] = piece.astype(F32)
        dst[own] = pad[...].astype(BF16)
    fold_own(g_attn, [w_qkv[:, a * width : (a + 1) * width] for a in range(3)] + [w_out[...]])
    fold_own(g_fc1, [w_fc1[:, a * width : (a + 1) * width] for a in range(4)])
    if height > 4 * part:
        fold_own(g_fc2, [w_fc2[a * part : (a + 1) * part, :] for a in range(4)])
    else:
        g_fc2[own] = w_fc2[...]
    place.meet()

    refs = (g_vec, g_attn, g_fc1, g_fc2)
    parts = [Gather(place, ref, cut, send.at[i], recv.at[i]) for i, (ref, cut) in enumerate(zip(refs, (None, 0, 1, 0)))]
    urgent, rest = parts[:2], parts[2:]
    order = [0] + place.steps
    todo = [(p, "line", k) for k in order for p in rest]
    todo += [(p, "plane", k) for k in order for p in rest]
    todo += [(p, "corner", k) for k in order for p in rest]

    def some(count):
        for p, stage, k in todo[:count]:
            getattr(p, stage)(k)
        del todo[:count]

    for p in urgent:
        p.begin()
    for p in urgent:
        p.line(0)
    for p in rest:
        p.begin()
    for k in place.steps:
        for p in urgent:
            p.line(k)
    for k in order:
        for p in urgent:
            p.plane(k)
        some(2)
    for k in order:
        for p in urgent:
            p.corner(k)
        some(2)
    for p in urgent:
        p.last()
    flat = lambda ref: [ref.at[j // 8, (j // 4) % 2, (j // 2) % 2, j % 2] for j in range(n)]
    unfold_vectors(flat(g_vec), vec, part)
    unfold(flat(g_attn), [wqkv.at[:, 0:width], wqkv.at[:, width : 2 * width], wqkv.at[:, 2 * width :], wout], part, height)

    def qkv_part(m, i):
        r = pl.ds(i * tile, tile)
        n1, _ = norm_rows(x_s[m, r, :].astype(F32))
        h1 = (n1 * vec[V_GAIN1 : V_GAIN1 + 1, 0:width] + vec[V_SHIFT1 : V_SHIFT1 + 1, 0:width]).astype(BF16)
        qkv_s[m, r, :] = (mm(h1, wqkv[...]) + vec[V_QKV : V_QKV + 1, 0 : 3 * width]).astype(BF16)

    stores = [pltpu.make_async_copy(qkv_s.at[m], qkv_ref.at[m], qkv_sem.at[m]) for m in range(micro)]
    turns = micro * (rows // tile)
    each = -(-len(todo) // max(turns, 1))
    for m in range(micro):
        loads[m].wait()
        for i in range(rows // tile):
            qkv_part(m, i)
            some(each)
        stores[m].start()
    some(len(todo))
    rest[0].last()
    unfold(flat(g_fc1), [w1.at[:, i * width : (i + 1) * width] for i in range(4)], part, height)
    rest[1].last()
    for p in parts:
        p.finish()
    for store in stores:
        store.wait()


def gather_call(n, x, w_qkv, w_out, w_fc1, w_fc2, small, collective_id, tile=512):
    micro, rows, width = x.shape
    height = -(-4 * w_out.shape[0] // 16) * 16
    vmem, hbm = pl.BlockSpec(memory_space=pltpu.VMEM), pl.BlockSpec(memory_space=pl.ANY)
    grid = (n // 8, 2, 2, 2)
    sems = pltpu.SemaphoreType.DMA((4, 6, n // 8))
    block = (height, width)
    shapes = [((micro, rows, 3 * width), BF16), ((width, 3 * width), BF16), ((width, width), BF16),
              ((width, 4 * width), BF16), (grid + block, BF16), ((8, 4 * width), F32)]
    return pl.pallas_call(
        functools.partial(gather_kernel, n, tile),
        in_specs=[hbm] + [vmem] * (4 + len(small)),
        out_specs=[hbm] + [vmem] * 5,
        out_shape=[jax.ShapeDtypeStruct(s, d) for s, d in shapes],
        scratch_shapes=[
            pltpu.VMEM(x.shape, BF16), pltpu.VMEM((micro, rows, 3 * width), BF16),
            pltpu.VMEM(grid + block, BF16), pltpu.VMEM(grid + block, BF16), pltpu.VMEM(grid + (16, 128), BF16),
            pltpu.VMEM(block, F32), pltpu.VMEM((16, 128), F32),
            pltpu.SemaphoreType.DMA((micro,)), pltpu.SemaphoreType.DMA((micro,)), sems, sems,
        ],
        compiler_params=pltpu.CompilerParams(
            collective_id=collective_id, has_side_effects=True, vmem_limit_bytes=60 * 2**20),
    )(x, w_qkv, w_out, w_fc1, w_fc2, *small)


def scatter_kernel(
    n, tile, x_ref, gqkv_ref, gmix_ref, wqkv, vec, p_fc1, p_fc2, p_out, gvec,
    ig_ref, o_attn, o_fc1, o_fc2, o_vec,
    x_s, gqkv_s, gmix_s, ig_s, h1_s, acc, acc_vec, p_attn, p_vec, in_sem, out_sem, send, recv, *rest,
):
    place = Place(n)
    micro, rows, width = x_s.shape
    part = width // n
    height = p_fc1.shape[-2]
    loads = []
    for m in range(micro):
        pairs = ((x_ref, x_s), (gqkv_ref, gqkv_s), (gmix_ref, gmix_s))
        loads.append([pltpu.make_async_copy(a.at[m], b.at[m], in_sem.at[i, m]) for i, (a, b) in enumerate(pairs)])
        for load in loads[m]:
            load.start()
    place.meet()

    def stream(i, src, cut, out):
        return Scatter(place, src, cut, rest[7 * i : 7 * i + 7], out, send.at[i], recv.at[i])
    fc = [stream(0, p_fc1, 0, o_fc1), stream(1, p_fc2, 1, o_fc2)]
    attn, vecs = stream(2, p_attn, 0, o_attn), stream(3, p_vec, None, o_vec)
    order = place.steps + [0]
    def stages(streams):
        return [(s, stage, k) for stage in ("corner", "plane", "line") for k in order for s in streams]
    todo = stages(fc)

    def some(count):
        for s, stage, k in todo[:count]:
            getattr(s, stage)(k)
        del todo[:count]

    for s in fc:
        s.begin()

    def v(i, cols=width):
        return vec[i : i + 1, 0:cols]

    acc_vec[...] = gvec[...]
    for m in range(micro):
        for load in loads[m][:2]:
            load.wait()
        for i in range(rows // tile):
            r = pl.ds(i * tile, tile)
            n1, _ = norm_rows(x_s[m, r, :].astype(F32))
            h1_s[m, r, :] = (n1 * v(V_GAIN1) + v(V_SHIFT1)).astype(BF16)
        g = t_mm(h1_s[m], gqkv_s[m])
        acc[...] = g if m == 0 else acc[...] + g
        some(len(order) * 2 if m == 0 else len(order))
    flat = lambda ref: [ref.at[j // 8, (j // 4) % 2, (j // 2) % 2, j % 2] for j in range(n)]
    fold([acc.at[:, 0:width], acc.at[:, width : 2 * width], acc.at[:, 2 * width :], p_out], flat(p_attn), part, height)
    attn.begin()
    late = stages([attn])
    todo = [t for pair in zip(todo, late) for t in pair] + todo[len(late) :] + late[len(todo) :]

    stores = [pltpu.make_async_copy(ig_s.at[m], ig_ref.at[m], out_sem.at[m]) for m in range(micro)]
    turns = micro * (rows // tile)
    each = -(-len(todo) // turns)
    for m in range(micro):
        loads[m][2].wait()
        for i in range(rows // tile):
            r = pl.ds(i * tile, tile)
            gqkv = gqkv_s[m, r, :]
            gh1 = mm_t(gqkv, wqkv[...])
            n1, r1 = norm_rows(x_s[m, r, :].astype(F32))
            acc_vec[V_QKV : V_QKV + 1, 0 : 3 * width] += col_sum(gqkv.astype(F32))
            acc_vec[V_GAIN1 : V_GAIN1 + 1, 0:width] += col_sum(gh1 * n1)
            acc_vec[V_SHIFT1 : V_SHIFT1 + 1, 0:width] += col_sum(gh1)
            ig_s[m, r, :] = (gmix_s[m, r, :] + norm_back(n1, r1, gh1 * v(V_GAIN1))).astype(BF16)
            some(each)
        stores[m].start()
    fold_vectors(acc_vec, flat(p_vec), part)
    vecs.begin()
    todo += stages([vecs])
    some(len(todo))
    for s in fc + [attn, vecs]:
        s.last()
    for s in fc + [attn, vecs]:
        s.finish()
    for store in stores:
        store.wait()


def scatter_call(n, x, gqkv, gmix, wqkv, vec, p_fc1, p_fc2, p_out, gvec, collective_id, tile=512):
    micro, rows, width = x.shape
    height = p_fc1.shape[0] // n
    vmem, hbm = pl.BlockSpec(memory_space=pltpu.VMEM), pl.BlockSpec(memory_space=pl.ANY)
    places = n // 8
    grid = (places, 2, 2, 2)
    scratch = []
    for shape, dtype in [((height, width), BF16)] * 3 + [((16, 128), F32)]:
        scratch += [pltpu.VMEM((places, 2, 2) + shape, dtype)]
        scratch += [pltpu.VMEM((places,) + shape, dtype) for _ in range(5)]
        scratch += [pltpu.VMEM((4, places) + shape, dtype)]
    block = jax.ShapeDtypeStruct((height, width), F32)
    sems = pltpu.SemaphoreType.DMA((4, 6, places))
    return pl.pallas_call(
        functools.partial(scatter_kernel, n, tile),
        in_specs=[hbm] * 3 + [vmem] * 6,
        out_specs=[hbm] + [vmem] * 4,
        out_shape=[jax.ShapeDtypeStruct(x.shape, BF16), block, block, block, jax.ShapeDtypeStruct((16, 128), F32)],
        scratch_shapes=[
            pltpu.VMEM(x.shape, BF16), pltpu.VMEM(gqkv.shape, BF16), pltpu.VMEM(gmix.shape, F32), pltpu.VMEM(x.shape, BF16),
            pltpu.VMEM(x.shape, BF16), pltpu.VMEM((width, 3 * width), F32), pltpu.VMEM(vec.shape, F32),
            pltpu.VMEM(grid + (height, width), BF16), pltpu.VMEM(grid + (16, 128), F32),
            pltpu.SemaphoreType.DMA((3, micro)), pltpu.SemaphoreType.DMA((micro,)), sems, sems,
        ] + scratch,
        compiler_params=pltpu.CompilerParams(
            collective_id=collective_id, has_side_effects=True, vmem_limit_bytes=62 * 2**20),
    )(x, gqkv, gmix, wqkv, vec, p_fc1.reshape(grid + (height, width)), p_fc2.reshape(grid + (height, width)), p_out, gvec)


def finish_kernel(part, ig_in, s_attn, s_fc1, s_fc2, s_vec, ig, g_qkv, g_out, g_fc1, g_fc2, *rest):
    vectors, held, sems = rest[:9], rest[9], rest[10]
    width = s_attn.shape[1]
    micro, rows = held.shape[:2]
    cuts = [(m, pl.ds(h * (rows // 2), rows // 2)) for m in range(micro) for h in range(2)]
    loads = [pltpu.make_async_copy(ig_in.at[c], held.at[c], sems.at[0, i]) for i, c in enumerate(cuts)]
    stores = [pltpu.make_async_copy(held.at[c], ig.at[c], sems.at[1, i]) for i, c in enumerate(cuts)]
    for load in loads:
        load.start()
    for a in range(4):
        own = slice(a * part, (a + 1) * part)
        if a < 3:
            g_qkv[:, a * width : (a + 1) * width] = s_attn[own, :]
        else:
            g_out[...] = s_attn[own, :]
        g_fc1[:, a * width : (a + 1) * width] = s_fc1[own, :]
    g_fc2[...] = s_fc2[0 : 4 * part, :]
    for i in range(8):
        vectors[i][...] = s_vec[i, 0:part]
    vectors[8][...] = s_vec[8, 0 : 4 * part]
    for load, store in zip(loads, stores):
        load.wait()
        store.start()
    for store in stores:
        store.wait()


def finish_call(part, ig, s_attn, s_fc1, s_fc2, s_vec):
    width = s_attn.shape[1]
    vmem, hbm = pl.BlockSpec(memory_space=pltpu.VMEM), pl.BlockSpec(memory_space=pl.ANY)
    shapes = [(part, 3 * width), (part, width), (part, 4 * width), (4 * part, width)] + [(part,)] * 8 + [(4 * part,)]
    return pl.pallas_call(
        functools.partial(finish_kernel, part),
        in_specs=[hbm] + [vmem] * 4,
        out_specs=[hbm] + [vmem] * 13,
        out_shape=[jax.ShapeDtypeStruct(ig.shape, ig.dtype)] + [jax.ShapeDtypeStruct(s, F32) for s in shapes],
        scratch_shapes=[pltpu.VMEM(ig.shape, ig.dtype), pltpu.SemaphoreType.DMA((2, 2 * ig.shape[0]))],
    )(ig, s_attn, s_fc1, s_fc2, s_vec)


def body(inputs, cotangent, w_qkv, w_out, w_fc1, w_fc2, gain1, shift1, q_bias, v_bias, out_bias, gain2, shift2,
         fc1_bias, fc2_bias, image_tokens, image_count):
    n = lax.axis_size("dp")
    part, width = w_out.shape
    hidden = w_fc1.shape[1]
    high = -(-4 * part // 16) * 16
    small = (gain1, shift1, q_bias, v_bias, out_bias, gain2, shift2, fc2_bias, fc1_bias)
    qkv, wqkv, wout, w1, g_fc2, vec = gather_call(n, inputs, w_qkv, w_out, w_fc1, w_fc2, small, 1)
    w2 = g_fc2.reshape(n, high, width)[:, : 4 * part].reshape(hidden, width)
    out, gqkv, gmix, p_fc1, p_fc2, a_out, a_vec = layer_call(
        image_tokens, image_count, inputs, cotangent, qkv, wout, w1, w2, vec, n)
    p_fc2 = jnp.pad(p_fc2.reshape(n, 4 * part, width), ((0, 0), (0, high - 4 * part), (0, 0))).reshape(n * high, width)
    ig, s_attn, s_fc1, s_fc2, s_vec = scatter_call(
        n, inputs, gqkv, gmix, wqkv, vec, p_fc1, p_fc2, a_out, a_vec, 2)
    ig, g_qkv, g_out, g_fc1, g_fc2, *v = finish_call(part, ig, s_attn, s_fc1, s_fc2, s_vec)
    return (out, ig, g_qkv, g_out, g_fc1, g_fc2, *v[:7], v[8], v[7])


def solution(mesh):
    big, mat, one = P(None, "dp", None), P("dp", None), P("dp")
    return jax.shard_map(
        body, mesh=mesh,
        in_specs=(big, big) + (mat,) * 4 + (one,) * 9 + (P(), P()),
        out_specs=(big, big) + (mat,) * 4 + (one,) * 9,
        check_vma=False,
    )
```

profile of v0, /device:TPU:0, one launch (start us, length us, event | category | flops | bytes accessed | tf_op | source)
XLA Modules:
  0.0 157.5 jit_solution(8789967960617729207)
XLA Ops:
  0.7 35.8 %shard_map.280 = (bf16[3,1024,1152]{2,1,0:T(8,128)(2,1)}, bf16[384,1152]{1,0:T(8,128)(2,1)}, bf16[384,384]{1,0:T(8,128)(2,1)}, bf16[384,1536]{1,0:T(8,128)(2,1)}...) custom-call(bf16[3,1024,384]{2,1,0:T(8,128)(2,1)} %x_ref.5, bf16[12,1152]{1,0:T(8,128)(2,1)} %w_qkv.1, ...), custom_call_target="tpu_custom_call" | custom-call | tf_op jit(solution)/shard_map/pallas_call | solution.py:636
  36.5 78.0 %shard_map.281 = (bf16[3,1024,384]{2,1,0:T(8,128)(2,1)}, bf16[3,1024,1152]{2,1,0:T(8,128)(2,1)}, f32[3,1024,384]{2,1,0:T(8,128)}, bf16[1536,384]{1,0:T(8,128)(2,...) custom-call(s32[3,32]{1,0:T(4,128)} %tokens.1, s32[3,32]{1,0:T(4,128)} %counts.1, ...), custom_call_target="tpu_custom_call" | custom-call | tf_op jit(solution)/shard_map/pallas_call | solution.py:340
  114.5 38.6 %shard_map.282 = (bf16[3,1024,384]{2,1,0:T(8,128)(2,1)}, f32[48,384]{1,0:T(8,128)}, f32[48,384]{1,0:T(8,128)}, f32[48,384]{1,0:T(8,128)}, f32[16,128]{1,0:T(8,128)}) custom-call(bf16[3,1024,384]{2,1,0:T(8,128)(2,1)} %x_ref.5, bf16[3,1024,1152]{2,1,0:T(8,128)(2,1)} %get-tuple-element.53.gqkv_ref, f32[3,1024,384]{2,1,0:T(8,128)} %get-tuple-element.54.gmix_ref, ...), custom_call_target="tpu_custom_call" | custom-call | tf_op jit(solution)/shard_map/pallas_call | solution.py:747
  153.1 4.2 %shard_map.283 = (bf16[3,1024,384]{2,1,0:T(8,128)(2,1)}, f32[12,1152]{1,0:T(8,128)}, f32[12,384]{1,0:T(8,128)}, f32[12,1536]{1,0:T(8,128)}, f32[48,384]{1,0:T(8,...) custom-call(bf16[3,1024,384]{2,1,0:T(8,128)(2,1)} %get-tuple-element, ...), custom_call_target="tpu_custom_call" | custom-call | tf_op jit(solution)/shard_map/pallas_call | solution.py:794
where the time goes:
time: 159 us; the launch traced here: 158 us
  Pallas kernels  157 us (99%)
    pallas_call x1, Pallas kernels, layer_call(): pl.pallas_call(functools.partial(layer_kernel, part=part, **kw), grid=(mi...  78 us
    pallas_call x1, Pallas kernels, scatter_call(): pl.pallas_call(functools.partial(scatter_kernel, n, tile), in_specs=[hbm]...  38.6 us
    pallas_call x1, Pallas kernels, gather_call(): pl.pallas_call(functools.partial(gather_kernel, n, tile), in_specs=[hbm]...  35.8 us
    pallas_call x1, Pallas kernels, finish_call(): pl.pallas_call(functools.partial(finish_kernel, part), in_specs=[hbm] + [...  4.19 us

commit v1 on v0

--- a/solution.py
+++ b/solution.py
@@ -228,9 +228,9 @@
 
 
 def layer_kernel(
-    tokens, counts, x_ref, cot_ref, qkv_ref, wout, w1, w2, vec,
-    out_ref, gqkv_ref, gmix_ref, p_fc1, p_fc2, a_out, a_vec,
-    a_fc1, a_fc2, o_s, inv_s, e1_s, e2_s, h2_s, act_s, gpre_s, gy_s, gb_s, go_s,
+    tokens, counts, x_ref, cot_ref, qkv_ref, wout_ref, w1_ref, w2_ref, vec,
+    out_ref, gqkv_ref, gmix_ref, p_fc1_ref, p_fc2_ref, a_out, a_vec,
+    wout, w1, w2, p_fc1, p_fc2, sems, a_fc1, a_fc2, o_s, inv_s, e1_s, e2_s, h2_s, act_s, gpre_s, gy_s, gb_s, go_s,
     part, phases=("af", "mlp", "wg", "ab"), tile=512, chunk=256,
 ):
     m = pl.program_id(0)
@@ -243,8 +243,20 @@
     total = length * count
     qkv_s, gqkv_s, gmix_s = qkv_ref.at[0], gqkv_ref.at[0], gmix_ref.at[0]
 
+    loads = [
+        pltpu.make_async_copy(a, b, sems.at[i])
+        for i, (a, b) in enumerate(((wout_ref, wout), (w1_ref, w1), (w2_ref, w2)))
+    ]
+    stores = [
+        pltpu.make_async_copy(a, b, sems.at[3 + i])
+        for i, (a, b) in enumerate(((p_fc1, p_fc1_ref), (p_fc2, p_fc2_ref)))
+    ]
+    final_step = m == pl.num_programs(0) - 1
+
     @pl.when(m == 0)
     def _():
+        for load in loads:
+            load.start()
         for ref in (a_out, a_fc1, a_fc2, a_vec):
             ref[...] = jnp.zeros_like(ref)
 
@@ -264,6 +276,11 @@
         @pl.when(length <= 256)
         def _():
             fwd(e2_s, *NARROW, pairs, width)
+
+    @pl.when(m == 0)
+    def _():
+        for load in loads:
+            load.wait()
 
     if "mlp" in phases:
         def mlp(i, c):
@@ -305,6 +322,15 @@
         a_fc2[...] += t_mm(act_s[...], gy_s[...])
         a_out[...] += t_mm(o_s[...], gb_s[...])
 
+    @pl.when(final_step)
+    def _():
+        high = p_fc1.shape[0] // (width // part)
+        blocks = [p_fc1.at[j * high : (j + 1) * high, :] for j in range(width // part)]
+        fold([a_fc1.at[:, i * width : (i + 1) * width] for i in range(4)], blocks, part, high)
+        p_fc2[...] = a_fc2[...].astype(BF16)
+        for store in stores:
+            store.start()
+
     gqkv_s[:, : 2 * width] = jnp.zeros((rows, 2 * width), BF16)
     gqkv_s[:, 2 * width :] = go_s[...]
 
@@ -317,12 +343,10 @@
         def _():
             bwd(e2_s, go_s, gqkv_s, *NARROW, pairs, width)
 
-    @pl.when(m == pl.num_programs(0) - 1)
+    @pl.when(final_step)
     def _():
-        high = p_fc1.shape[0] // (width // part)
-        blocks = [p_fc1.at[j * high : (j + 1) * high, :] for j in range(width // part)]
-        fold([a_fc1.at[:, i * width : (i + 1) * width] for i in range(4)], blocks, part, high)
-        p_fc2[...] = a_fc2[...].astype(BF16)
+        for store in stores:
+            store.wait()
 
 
 def layer_call(tokens, counts, x, cot, qkv, wout, w1, w2, vec, n, **kw):
@@ -334,6 +358,7 @@
         return pl.BlockSpec((1, rows, cols), lambda m: (m, 0, 0))
     def whole(shape):
         return pl.BlockSpec(shape, lambda m: (0, 0), pipeline_mode=pl.Buffered(1))
+    hbm = pl.BlockSpec(memory_space=pl.ANY)
     bf = lambda n: pltpu.VMEM((rows, n), BF16)
     outs = [(x.shape, BF16), ((micro, rows, 3 * width), BF16), (x.shape, F32)]
     kept = [((n * high, width), BF16), ((hidden, width), BF16), ((width, width), F32), (vec.shape, F32)]
@@ -341,10 +366,11 @@
         functools.partial(layer_kernel, part=part, **kw),
         grid=(micro,),
         in_specs=[pl.BlockSpec(memory_space=pltpu.SMEM)] * 2 + [per_step(width), per_step(width), per_step(3 * width)]
-        + [whole(a.shape) for a in (wout, w1, w2, vec)],
-        out_specs=[per_step(s[2]) for s, _ in outs] + [whole(s) for s, _ in kept],
+        + [hbm] * 3 + [whole(vec.shape)],
+        out_specs=[per_step(s[2]) for s, _ in outs] + [hbm] * 2 + [whole(s) for s, _ in kept[2:]],
         out_shape=[jax.ShapeDtypeStruct(s, d) for s, d in outs + kept],
-        scratch_shapes=[
+        scratch_shapes=[pltpu.VMEM(a.shape, BF16) for a in (wout, w1, w2)] + [
+            pltpu.VMEM(kept[0][0], BF16), pltpu.VMEM(kept[1][0], BF16), pltpu.SemaphoreType.DMA((5,)),
             pltpu.VMEM((width, hidden), F32), pltpu.VMEM((hidden, width), F32),
             bf(width), pltpu.VMEM((rows, width), F32),
             pltpu.VMEM((9, 352, 768), BF16), pltpu.VMEM((15, 224, 512), BF16),
@@ -580,19 +606,19 @@
         p.begin()
     for p in urgent:
         p.line(0)
-    for p in rest:
-        p.begin()
     for k in place.steps:
         for p in urgent:
             p.line(k)
+    for p in rest:
+        p.begin()
     for k in order:
         for p in urgent:
             p.plane(k)
-        some(2)
+        some(1)
     for k in order:
         for p in urgent:
             p.corner(k)
-        some(2)
+        some(1)
     for p in urgent:
         p.last()
     flat = lambda ref: [ref.at[j // 8, (j // 4) % 2, (j // 2) % 2, j % 2] for j in range(n)]
@@ -652,7 +678,7 @@
 def scatter_kernel(
     n, tile, x_ref, gqkv_ref, gmix_ref, wqkv, vec, p_fc1, p_fc2, p_out, gvec,
     ig_ref, o_attn, o_fc1, o_fc2, o_vec,
-    x_s, gqkv_s, gmix_s, ig_s, h1_s, acc, acc_vec, p_attn, p_vec, in_sem, out_sem, send, recv, *rest,
+    x_s, gqkv_s, gmix_s, ig_s, n1_s, acc, acc_vec, p_attn, p_vec, in_sem, out_sem, send, recv, *rest,
 ):
     place = Place(n)
     micro, rows, width = x_s.shape
@@ -693,14 +719,30 @@
         for i in range(rows // tile):
             r = pl.ds(i * tile, tile)
             n1, _ = norm_rows(x_s[m, r, :].astype(F32))
-            h1_s[m, r, :] = (n1 * v(V_GAIN1) + v(V_SHIFT1)).astype(BF16)
-        g = t_mm(h1_s[m], gqkv_s[m])
+            n1_s[m, r, :] = n1.astype(BF16)
+        g = t_mm(n1_s[m], gqkv_s[m])
         acc[...] = g if m == 0 else acc[...] + g
+        acc_vec[V_QKV : V_QKV + 1, 0 : 3 * width] += col_sum(gqkv_s[m].astype(F32))
         some(len(order) * 2 if m == 0 else len(order))
+    total = acc[...]
+    sums = acc_vec[V_QKV : V_QKV + 1, 0 : 3 * width]
+    table = jnp.concatenate([jnp.broadcast_to(v(V_GAIN1), (64, width)), jnp.broadcast_to(v(V_SHIFT1), (64, width))], axis=0)
+    table = jnp.transpose(table)
+    acc[...] = total * table[:, 0:1] + sums * table[:, 64:65]
     flat = lambda ref: [ref.at[j // 8, (j // 4) % 2, (j // 2) % 2, j % 2] for j in range(n)]
     fold([acc.at[:, 0:width], acc.at[:, width : 2 * width], acc.at[:, 2 * width :], p_out], flat(p_attn), part, height)
     attn.begin()
-    late = stages([attn])
+    dots = jnp.sum(wqkv[...].astype(F32) * total, axis=1, keepdims=True)
+    acc_vec[V_GAIN1 : V_GAIN1 + 1, 0:width] += jnp.transpose(jnp.broadcast_to(dots, (width, 128)))[0:1, :]
+    one = sums.astype(BF16).astype(F32)
+    two = (sums - one).astype(BF16).astype(F32)
+    three = sums - one - two
+    row = lax.broadcasted_iota(jnp.int32, (16, 3 * width), 0)
+    split = jnp.where(row == 0, one, jnp.where(row == 1, two, jnp.where(row == 2, three, 0.0))).astype(BF16)
+    acc_vec[V_SHIFT1 : V_SHIFT1 + 1, 0:width] += col_sum(mm_t(split, wqkv[...]))
+    fold_vectors(acc_vec, flat(p_vec), part)
+    vecs.begin()
+    late = [t for pair in zip(stages([attn]), stages([vecs])) for t in pair]
     todo = [t for pair in zip(todo, late) for t in pair] + todo[len(late) :] + late[len(todo) :]
 
     stores = [pltpu.make_async_copy(ig_s.at[m], ig_ref.at[m], out_sem.at[m]) for m in range(micro)]
@@ -713,15 +755,9 @@
             gqkv = gqkv_s[m, r, :]
             gh1 = mm_t(gqkv, wqkv[...])
             n1, r1 = norm_rows(x_s[m, r, :].astype(F32))
-            acc_vec[V_QKV : V_QKV + 1, 0 : 3 * width] += col_sum(gqkv.astype(F32))
-            acc_vec[V_GAIN1 : V_GAIN1 + 1, 0:width] += col_sum(gh1 * n1)
-            acc_vec[V_SHIFT1 : V_SHIFT1 + 1, 0:width] += col_sum(gh1)
             ig_s[m, r, :] = (gmix_s[m, r, :] + norm_back(n1, r1, gh1 * v(V_GAIN1))).astype(BF16)
             some(each)
         stores[m].start()
-    fold_vectors(acc_vec, flat(p_vec), part)
-    vecs.begin()
-    todo += stages([vecs])
     some(len(todo))
     for s in fc + [attn, vecs]:
         s.last()

time: 159 us -> 150 us (0.943)
  Pallas kernels: 157 us -> 149 us
    pallas_call x1, Pallas kernels: 78 us -> 74.6 us  [layer_call(): pl.pallas_call(functools.partial(layer_kernel, part=part, **kw), grid=(mi...]
    pallas_call x1, Pallas kernels: 35.8 us -> 33.6 us  [gather_call(): pl.pallas_call(functools.partial(gather_kernel, n, tile), in_specs=[hbm]...]
    pallas_call x1, Pallas kernels: 38.6 us -> 36.5 us  [scatter_call(): pl.pallas_call(functools.partial(scatter_kernel, n, tile), in_specs=[hbm]...]
where the time goes in v1:
time: 150 us
  Pallas kernels  149 us (99%)
    pallas_call x1, Pallas kernels, layer_call(): pl.pallas_call(functools.partial(layer_kernel, part=part, **kw), grid=(mi...  74.6 us
    pallas_call x1, Pallas kernels, scatter_call(): pl.pallas_call(functools.partial(scatter_kernel, n, tile), in_specs=[hbm]...  36.5 us
    pallas_call x1, Pallas kernels, gather_call(): pl.pallas_call(functools.partial(gather_kernel, n, tile), in_specs=[hbm]...  33.6 us
    pallas_call x1, Pallas kernels, finish_call(): pl.pallas_call(functools.partial(finish_kernel, part), in_specs=[hbm] + [...  4.19 us

profile of v1, /device:TPU:0, one launch (start us, length us, event | category | flops | bytes accessed | tf_op | source)
XLA Modules:
  0.0 149.7 jit_solution(8937628046098734216)
XLA Ops:
  0.7 33.6 %shard_map.280 = (bf16[3,1024,1152]{2,1,0:T(8,128)(2,1)}, bf16[384,1152]{1,0:T(8,128)(2,1)}, bf16[384,384]{1,0:T(8,128)(2,1)}, bf16[384,1536]{1,0:T(8,128)(2,1)}...) custom-call(bf16[3,1024,384]{2,1,0:T(8,128)(2,1)} %x_ref.5, bf16[12,1152]{1,0:T(8,128)(2,1)} %w_qkv.1, ...), custom_call_target="tpu_custom_call" | custom-call | tf_op jit(solution)/shard_map/pallas_call | solution.py:662
  34.2 74.6 %shard_map.281 = (bf16[3,1024,384]{2,1,0:T(8,128)(2,1)}, bf16[3,1024,1152]{2,1,0:T(8,128)(2,1)}, f32[3,1024,384]{2,1,0:T(8,128)}, bf16[1536,384]{1,0:T(8,128)(2,...) custom-call(s32[3,32]{1,0:T(4,128)} %tokens.1, s32[3,32]{1,0:T(4,128)} %counts.1, ...), custom_call_target="tpu_custom_call" | custom-call | tf_op jit(solution)/shard_map/pallas_call | solution.py:365
  108.9 36.5 %shard_map.282 = (bf16[3,1024,384]{2,1,0:T(8,128)(2,1)}, f32[48,384]{1,0:T(8,128)}, f32[48,384]{1,0:T(8,128)}, f32[48,384]{1,0:T(8,128)}, f32[16,128]{1,0:T(8,128)}) custom-call(bf16[3,1024,384]{2,1,0:T(8,128)(2,1)} %x_ref.5, bf16[3,1024,1152]{2,1,0:T(8,128)(2,1)} %get-tuple-element.53.gqkv_ref, f32[3,1024,384]{2,1,0:T(8,128)} %get-tuple-element.54.gmix_ref, ...), custom_call_target="tpu_custom_call" | custom-call | tf_op jit(solution)/shard_map/pallas_call | solution.py:783
  145.3 4.2 %shard_map.283 = (bf16[3,1024,384]{2,1,0:T(8,128)(2,1)}, f32[12,1152]{1,0:T(8,128)}, f32[12,384]{1,0:T(8,128)}, f32[12,1536]{1,0:T(8,128)}, f32[48,384]{1,0:T(8,...) custom-call(bf16[3,1024,384]{2,1,0:T(8,128)(2,1)} %get-tuple-element, ...), custom_call_target="tpu_custom_call" | custom-call | tf_op jit(solution)/shard_map/pallas_call | solution.py:830

commit v2 on v1

--- a/solution.py
+++ b/solution.py
@@ -319,7 +319,7 @@
 
     if "wg" in phases:
         a_fc1[...] += t_mm(h2_s[...], gpre_s[...])
-        a_fc2[...] += t_mm(act_s[...], gy_s[...])
+        a_fc2[...] += t_mm(gy_s[...], act_s[...])
         a_out[...] += t_mm(o_s[...], gb_s[...])
 
     @pl.when(final_step)
@@ -327,7 +327,8 @@
         high = p_fc1.shape[0] // (width // part)
         blocks = [p_fc1.at[j * high : (j + 1) * high, :] for j in range(width // part)]
         fold([a_fc1.at[:, i * width : (i + 1) * width] for i in range(4)], blocks, part, high)
-        p_fc2[...] = a_fc2[...].astype(BF16)
+        for i in range(0, hidden, 128):
+            p_fc2[i : i + 128, :] = jnp.transpose(a_fc2[:, i : i + 128]).astype(BF16)
         for store in stores:
             store.start()
 
@@ -371,7 +372,7 @@
         out_shape=[jax.ShapeDtypeStruct(s, d) for s, d in outs + kept],
         scratch_shapes=[pltpu.VMEM(a.shape, BF16) for a in (wout, w1, w2)] + [
             pltpu.VMEM(kept[0][0], BF16), pltpu.VMEM(kept[1][0], BF16), pltpu.SemaphoreType.DMA((5,)),
-            pltpu.VMEM((width, hidden), F32), pltpu.VMEM((hidden, width), F32),
+            pltpu.VMEM((width, hidden), F32), pltpu.VMEM((width, hidden), F32),
             bf(width), pltpu.VMEM((rows, width), F32),
             pltpu.VMEM((9, 352, 768), BF16), pltpu.VMEM((15, 224, 512), BF16),
             bf(width), bf(hidden), bf(hidden), bf(width), bf(width), bf(width),
@@ -631,15 +632,20 @@
         h1 = (n1 * vec[V_GAIN1 : V_GAIN1 + 1, 0:width] + vec[V_SHIFT1 : V_SHIFT1 + 1, 0:width]).astype(BF16)
         qkv_s[m, r, :] = (mm(h1, wqkv[...]) + vec[V_QKV : V_QKV + 1, 0 : 3 * width]).astype(BF16)
 
-    stores = [pltpu.make_async_copy(qkv_s.at[m], qkv_ref.at[m], qkv_sem.at[m]) for m in range(micro)]
-    turns = micro * (rows // tile)
+    pieces = rows // tile
+    stores = []
+    for m in range(micro):
+        for i in range(pieces):
+            where = (m, pl.ds(i * tile, tile))
+            stores.append(pltpu.make_async_copy(qkv_s.at[where], qkv_ref.at[where], qkv_sem.at[m, i]))
+    turns = micro * pieces
     each = -(-len(todo) // max(turns, 1))
     for m in range(micro):
         loads[m].wait()
         for i in range(rows // tile):
             qkv_part(m, i)
+            stores[m * pieces + i].start()
             some(each)
-        stores[m].start()
     some(len(todo))
     rest[0].last()
     unfold(flat(g_fc1), [w1.at[:, i * width : (i + 1) * width] for i in range(4)], part, height)
@@ -668,7 +674,7 @@
             pltpu.VMEM(x.shape, BF16), pltpu.VMEM((micro, rows, 3 * width), BF16),
             pltpu.VMEM(grid + block, BF16), pltpu.VMEM(grid + block, BF16), pltpu.VMEM(grid + (16, 128), BF16),
             pltpu.VMEM(block, F32), pltpu.VMEM((16, 128), F32),
-            pltpu.SemaphoreType.DMA((micro,)), pltpu.SemaphoreType.DMA((micro,)), sems, sems,
+            pltpu.SemaphoreType.DMA((micro,)), pltpu.SemaphoreType.DMA((micro, rows // tile)), sems, sems,
         ],
         compiler_params=pltpu.CompilerParams(
             collective_id=collective_id, has_side_effects=True, vmem_limit_bytes=60 * 2**20),

time: 150 us -> 149 us (level)
  no operation moved by 1% of the time
where the time goes in v2:
time: 149 us
  Pallas kernels  148 us (99%)
    pallas_call x1, Pallas kernels, layer_call(): pl.pallas_call(functools.partial(layer_kernel, part=part, **kw), grid=(mi...  73.8 us
    pallas_call x1, Pallas kernels, scatter_call(): pl.pallas_call(functools.partial(scatter_kernel, n, tile), in_specs=[hbm]...  36.4 us
    pallas_call x1, Pallas kernels, gather_call(): pl.pallas_call(functools.partial(gather_kernel, n, tile), in_specs=[hbm]...  33.6 us
    pallas_call x1, Pallas kernels, finish_call(): pl.pallas_call(functools.partial(finish_kernel, part), in_specs=[hbm] + [...  4.19 us

profile of v2, /device:TPU:0, one launch (start us, length us, event | category | flops | bytes accessed | tf_op | source)
XLA Modules:
  0.0 148.9 jit_solution(5589315497384859821)
XLA Ops:
  0.7 33.6 %shard_map.280 = (bf16[3,1024,1152]{2,1,0:T(8,128)(2,1)}, bf16[384,1152]{1,0:T(8,128)(2,1)}, bf16[384,384]{1,0:T(8,128)(2,1)}, bf16[384,1536]{1,0:T(8,128)(2,1)}...) custom-call(bf16[3,1024,384]{2,1,0:T(8,128)(2,1)} %x_ref.5, bf16[12,1152]{1,0:T(8,128)(2,1)} %w_qkv.1, ...), custom_call_target="tpu_custom_call" | custom-call | tf_op jit(solution)/shard_map/pallas_call | solution.py:668
  34.3 73.8 %shard_map.281 = (bf16[3,1024,384]{2,1,0:T(8,128)(2,1)}, bf16[3,1024,1152]{2,1,0:T(8,128)(2,1)}, f32[3,1024,384]{2,1,0:T(8,128)}, bf16[1536,384]{1,0:T(8,128)(2,...) custom-call(s32[3,32]{1,0:T(4,128)} %tokens.1, s32[3,32]{1,0:T(4,128)} %counts.1, ...), custom_call_target="tpu_custom_call" | custom-call | tf_op jit(solution)/shard_map/pallas_call | solution.py:366
  108.1 36.4 %shard_map.282 = (bf16[3,1024,384]{2,1,0:T(8,128)(2,1)}, f32[48,384]{1,0:T(8,128)}, f32[48,384]{1,0:T(8,128)}, f32[48,384]{1,0:T(8,128)}, f32[16,128]{1,0:T(8,128)}) custom-call(bf16[3,1024,384]{2,1,0:T(8,128)(2,1)} %x_ref.5, bf16[3,1024,1152]{2,1,0:T(8,128)(2,1)} %get-tuple-element.53.gqkv_ref, f32[3,1024,384]{2,1,0:T(8,128)} %get-tuple-element.54.gmix_ref, ...), custom_call_target="tpu_custom_call" | custom-call | tf_op jit(solution)/shard_map/pallas_call | solution.py:789
  144.5 4.2 %shard_map.283 = (bf16[3,1024,384]{2,1,0:T(8,128)(2,1)}, f32[12,1152]{1,0:T(8,128)}, f32[12,384]{1,0:T(8,128)}, f32[12,1536]{1,0:T(8,128)}, f32[48,384]{1,0:T(8,...) custom-call(bf16[3,1024,384]{2,1,0:T(8,128)(2,1)} %get-tuple-element, ...), custom_call_target="tpu_custom_call" | custom-call | tf_op jit(solution)/shard_map/pallas_call | solution.py:836
